TPU v7x, 32 devices: a whole 2x2x4 slice. The times are simulated.
32 devices in a mesh: freq: 8 (over z, x), bl: 4 (over y, core).
Axes of the slice: x: 2, y: 2, z: 4, core: 2. Of those that a mesh axis runs over, the one named last changes fastest.
Arguments:
- voltages: bfloat16 [1024, 134144], P(('bl', 'freq')), may hold values from -6 to 6
- fir_taps: float32 [4, 1024], replicated, may hold values from -3 to 3
- antenna_order: int32 [1024], replicated, may hold values from 0 to 1023, each once
- tile_list: int32 [4, 2], replicated, may hold values from 0 to 3
Outputs:
- visibilities: bfloat16 [4, 512, 256, 512], P('bl', 'freq')
All inputs are finite; a program needn't handle non-finite values.
Results may differ from a plain program's by a relative error of at most 0.0074.
Values may be sent and summed in bfloat16 or wider, within the bound.
A program may use at most 128 MiB of HBM per device.

v0:
```python
import math

import jax
import jax.numpy as jnp
from jax import lax
from jax.sharding import PartitionSpec as P

K = 1024
TAPS = 4
PANEL = 256
SAMPLES = 128


def make_table(points, kept):
    product = (
        jnp.arange(points, dtype=jnp.int32)[:, None]
        * jnp.arange(kept, dtype=jnp.int32)[None, :]
        % points
    )
    phase = 2.0 * math.pi / points * product.astype(jnp.float32)
    return jnp.concatenate([jnp.cos(phase), -jnp.sin(phase)], axis=1).astype(jnp.bfloat16)


def arrange(panel):
    width = panel.shape[1]
    return jnp.transpose(panel, (3, 0, 2, 1)).reshape(panel.shape[3], panel.shape[0], 2 * width)


def rotated(panel):
    turned = jnp.stack([-panel[:, :, 1, :], panel[:, :, 0, :]], axis=2)
    return arrange(turned)


def correlate(source, antenna_order, tile):
    row_ids = lax.dynamic_slice_in_dim(antenna_order, tile[0] * PANEL, PANEL)
    col_ids = lax.dynamic_slice_in_dim(antenna_order, tile[1] * PANEL, PANEL)
    row_panel = jnp.take(source, row_ids, axis=0)
    col_panel = jnp.take(source, col_ids, axis=0)
    left = arrange(row_panel)
    right = jnp.concatenate([arrange(col_panel), rotated(col_panel)], axis=1)
    return jnp.einsum("fps,fqs->fpq", left, right, preferred_element_type=jnp.float32)


def per_device(voltages, fir_taps, antenna_order, tile_list):
    local_count = voltages.shape[0]
    frames = voltages.reshape(local_count, SAMPLES + TAPS - 1, K)
    filtered = jnp.zeros((local_count, SAMPLES, K), jnp.float32)
    for tap in range(TAPS):
        filtered = filtered + fir_taps[tap][None, None, :] * frames[
            :, tap : tap + SAMPLES, :
        ].astype(jnp.float32)
    filtered = filtered.astype(jnp.bfloat16)
    table = make_table(K, K // 2)
    spectra = jnp.dot(
        filtered.reshape(local_count * SAMPLES, K), table, preferred_element_type=jnp.float32
    )
    spectra = (
        (spectra * (1.0 / math.sqrt(K)))
        .astype(jnp.bfloat16)
        .reshape(local_count, SAMPLES, 2, K // 2)
    )
    turned = lax.all_to_all(spectra, "freq", split_axis=3, concat_axis=0, tiled=True)
    gathered = lax.all_gather(turned, "bl", axis=0, tiled=True)
    own_tile = tile_list[lax.axis_index("bl")]
    summed = correlate(gathered, antenna_order, own_tile)
    return (summed / SAMPLES).astype(jnp.bfloat16)[None]


def solution(mesh):
    return jax.shard_map(
        per_device,
        mesh=mesh,
        in_specs=(P(("bl", "freq"), None), P(), P(), P()),
        out_specs=P("bl", "freq", None, None),
        check_vma=False,
    )
```

profile of v0, /device:TPU:10, one launch (start us, length us, event | category | flops | bytes accessed | tf_op | source)
XLA Modules:
  0.0 655.1 jit_solution(10840728497448380260)
XLA Ops:
  6.5 0.0 copy-start
  6.5 0.0 all-gather.2.cloned.1.call-start
  6.5 8.5 %negate_convert_fusion = (bf16[1024,512]{1,0:T(8,128)(2,1)S(1)}, bf16[1024,512]{1,0:T(8,128)(2,1)S(1)}) fusion(), kind=kLoop, calls=%fused_computation.23 | loop fusion | flops 8912896 | bytes 2097152 | tf_op jit(solution)/shard_map/convert.1
  15.1 0.0 copy-start.2
  15.1 9.2 %reshape.35 = bf16[32,131,1024]{2,1,0:T(8,128)(2,1)} reshape(bf16[32,134144]{1,0:T(8,128)(2,1)} %param.6) | data formatting | bytes 17170432 | tf_op jit(solution)/shard_map/reshape | solution.py:46
  24.3 0.0 copy-done.2
  24.3 19.3 %add_convert_fusion = bf16[32,128,1024]{2,1,0:T(8,128)(2,1)S(1)} fusion(bf16[32,131,1024]{2,1,0:T(8,128)(2,1)} %reshape.35, f32[1024]{0:T(1024)S(1)} %bitcast.28, f32[1024]{0:T(1024)S(1)} %bitcast.29, f32[1024]{0:T(1024)S(1)} %bitcast.27, f32[1024]{0:T(1024)S(1)} %bitcast.26), kind=kLoop, calls=%fused_computation.9 | loop fusion | flops 50331648 | bytes 41959424 | tf_op jit(solution)/shard_map/convert_element_type | solution.py:52
  43.6 11.0 %multiply_convert_fusion.1 = bf16[4096,1024]{1,0:T(8,128)(2,1)} fusion(bf16[4096,1024]{1,0:T(8,128)(2,1)S(1)} %bitcast.24, bf16[1024,512]{1,0:T(8,128)(2,1)S(1)} %get-tuple-element.20, bf16[1024,512]{1,0:T(8,128)(2,1)S(1)} %get-tuple-element.21), kind=kOutput, calls=%fused_computation.8 | convolution fusion | flops 8602517504 | bytes 18874368 | tf_op jit(solution)/shard_map/dot_general | solution.py:54
  54.6 14.5 %reshape.37 = bf16[32,128,2,512]{3,2,1,0:T(2,128)(2,1)} reshape(bf16[4096,1024]{1,0:T(8,128)(2,1)} %multiply_convert_fusion.1) | data formatting | bytes 16777216 | tf_op jit(solution)/shard_map/reshape | solution.py:60
  69.1 28.1 %copy.15 = bf16[32,128,2,512]{1,2,0,3:T(2,128)(2,1)} copy(bf16[32,128,2,512]{3,2,1,0:T(2,128)(2,1)} %reshape.37) | data formatting | bytes 16777216 | tf_op jit(solution)/shard_map/reshape | solution.py:60
  97.2 187.3 %all_to_all.18 = bf16[32,128,2,512]{1,2,0,3:T(2,128)(2,1)} all-to-all(bf16[32,128,2,512]{1,2,0,3:T(2,128)(2,1)} %copy.15), channel_id=1, replica_groups=mesh['freq'=8,'bl'=4] {'freq'}, dimensions={3} | all-to-all | bytes 16777216 | tf_op jit(solution)/shard_map/all_to_all | solution.py:62
  284.4 16.5 %copy.16 = bf16[32,128,2,512]{1,3,2,0:T(8,128)(2,1)} copy(bf16[32,128,2,512]{1,2,0,3:T(2,128)(2,1)} %all_to_all.18) | data formatting | bytes 16777216 | tf_op jit(solution)/shard_map/all_to_all | solution.py:62
  300.9 9.8 %copy.17 = bf16[8,32,128,2,64]{2,4,3,1,0:T(8,128)(2,1)} copy(bf16[8,32,128,2,64]{2,4,0,3,1:T(8,128)(2,1)} %bitcast.23) | data formatting | bytes 16777216 | tf_op jit(solution)/shard_map/all_to_all | solution.py:62
  310.8 0.0 copy-start.3
  310.8 0.0 all-gather.2.cloned.1.call-update
  310.8 0.0 copy-done
  310.8 0.1 constant_dynamic-slice_fusion
  310.9 0.5 fusion.19
  312.7 0.0 copy-done.3
  312.7 0.1 compare_and_fusion
  312.8 200.4 %all-gather.2.cloned.1.call-done = bf16[1024,128,2,64]{1,3,2,0:T(8,128)(2,1)} async-done(((bf16[256,128,2,64]{1,3,2,0:T(8,128)(2,1)}), bf16[1024,128,2,64]{1,3,2,0:T(8,128)(2,1)}) %all-gather.2.cloned.1.call-update) | async-done | bytes 33554448 | tf_op jit(solution)/shard_map/all_gather | solution.py:63
  513.2 9.1 %gather_fusion.1 = bf16[256,128,2,64]{1,3,2,0:T(8,128)(2,1)} fusion(bf16[1024,128,2,64]{1,3,2,0:T(8,128)(2,1)} %all-gather.2.cloned.1.call-done, s32[1024]{0:T(1024)S(1)} %get-tuple-element.22), kind=kCustom, calls=%fused_computation.1.clone | custom fusion | bytes 16778240 | tf_op jit(solution)/shard_map/jit(_take)/gather | solution.py:38
  522.3 7.4 %broadcast_select_fusion = bf16[256,128,2,64]{1,3,2,0:T(8,128)(2,1)} fusion(bf16[256,128,2,64]{1,3,2,0:T(8,128)(2,1)} %gather_fusion.1, pred[256]{0:T(512)(128)(4,1)S(1)} %get-tuple-element.6), kind=kLoop, calls=%fused_computation.12 | loop fusion | flops 4194304 | bytes 16777472 | tf_op jit(solution)/shard_map/jit(_take)/select_n | solution.py:38
  529.7 7.4 %fusion.22 = bf16[64,256,2,128]{3,0,2,1:T(8,128)(2,1)} fusion(bf16[256,128,2,64]{1,3,2,0:T(8,128)(2,1)} %gather_fusion.1, pred[256]{0:T(512)(128)(4,1)S(1)} %get-tuple-element.6), kind=kLoop, calls=%fused_computation.39 | loop fusion | flops 4194304 | bytes 16777472 | tf_op jit(solution)/shard_map/transpose | solution.py:26
  537.1 9.1 %gather_fusion = bf16[256,128,2,64]{1,3,2,0:T(8,128)(2,1)} fusion(bf16[1024,128,2,64]{1,3,2,0:T(8,128)(2,1)} %all-gather.2.cloned.1.call-done, s32[1024]{0:T(1024)S(1)} %get-tuple-element.23), kind=kCustom, calls=%fused_computation.clone | custom fusion | bytes 16778240 | tf_op jit(solution)/shard_map/jit(_take)/gather | solution.py:37
  546.2 7.6 %select_bitcast_fusion = bf16[64,256,2,128]{3,0,2,1:T(8,128)(2,1)} fusion(bf16[256,128,2,64]{1,3,2,0:T(8,128)(2,1)} %gather_fusion, pred[256]{0:T(512)(128)(4,1)S(1)} %get-tuple-element.16), kind=kLoop, calls=%fused_computation.11 | loop fusion | flops 4194304 | bytes 16777472 | tf_op jit(solution)/shard_map/transpose | solution.py:26
  553.8 12.9 %copy.18 = bf16[64,256,2,128]{1,3,2,0:T(8,128)(2,1)} copy(bf16[64,256,2,128]{3,0,2,1:T(8,128)(2,1)} %select_bitcast_fusion) | data formatting | bytes 16777216 | tf_op jit(solution)/shard_map/transpose | solution.py:26
  566.8 5.2 slice_negate_fusion
  572.0 6.5 maximum_bitcast_fusion
  578.5 13.2 %copy.20 = bf16[64,256,2,128]{3,2,1,0:T(2,128)(2,1)} copy(bf16[64,256,2,128]{3,0,2,1:T(8,128)(2,1)} %maximum_bitcast_fusion) | data formatting | bytes 16777216 | tf_op jit(solution)/shard_map/transpose | solution.py:26
  591.6 14.1 %reshape.40 = bf16[64,256,256]{2,1,0:T(8,128)(2,1)} reshape(bf16[64,256,2,128]{3,2,1,0:T(2,128)(2,1)} %copy.20) | data formatting | bytes 16777216 | tf_op jit(solution)/shard_map/reshape | solution.py:26
  605.7 13.2 %copy.19 = bf16[64,256,2,128]{3,2,1,0:T(2,128)(2,1)} copy(bf16[64,256,2,128]{3,0,2,1:T(8,128)(2,1)} %fusion.22) | data formatting | bytes 16777216 | tf_op jit(solution)/shard_map/transpose | solution.py:26
  618.9 14.1 %reshape.39 = bf16[64,256,256]{2,1,0:T(8,128)(2,1)} reshape(bf16[64,256,2,128]{3,2,1,0:T(2,128)(2,1)} %copy.19) | data formatting | bytes 16777216 | tf_op jit(solution)/shard_map/reshape | solution.py:26
  633.0 0.0 copy-start.1
  633.0 15.2 %fusion = bf16[1,64,256,512]{3,2,1,0:T(8,128)(2,1)} fusion(bf16[64,256,256]{1,2,0:T(8,128)(2,1)} %bitcast.25, bf16[64,256,256]{2,1,0:T(8,128)(2,1)} %reshape.40, bf16[64,256,256]{2,1,0:T(8,128)(2,1)} %reshape.39), kind=kOutput, calls=%fused_computation.3 | convolution fusion | flops 4345298944 | bytes 41943040 | tf_op jit(solution)/shard_map/fps,fqs->fpq/dot_general | solution.py:41
  648.2 0.0 copy-done.1
  (2 shorter events, 0.0 us)
Async XLA Ops:
  6.5 304.2 %copy-start = (s32[4,2]{0,1:T(2,128)S(1)}, s32[4,2]{0,1:T(2,128)}, u32[]{:S(2)}) copy-start(s32[4,2]{0,1:T(2,128)} %param.9) | copy-start | bytes 100
  6.5 506.6 %all-gather.2.cloned.1.call-start = ((), (), s32[]{:S(2)}) async-start(), calls=%async_computation.1 | async-start | bytes 41943040 | tf_op jit(solution)/shard_map/all_gather | solution.py:63
  15.1 9.2 %copy-start.2 = (f32[4,1024]{1,0:T(4,128)S(1)}, f32[4,1024]{1,0:T(4,128)}, u32[]{:S(2)}) copy-start(f32[4,1024]{1,0:T(4,128)} %param.7) | copy-start | bytes 49156
  310.8 1.9 copy-start.3
  633.0 15.2 %copy-start.1 = (s32[4,2]{0,1:T(2,128)S(1)}, s32[4,2]{0,1:T(2,128)}, u32[]{:S(2)}) copy-start(s32[4,2]{0,1:T(2,128)} %param.9) | copy-start | bytes 100
Sparse Core Ops, SparseCore 0:
  310.9 202.2 all-gather.1
where the time goes:
time: 659 us; the launch traced here: 655 us
  waiting for transfers between devices  200 us (30%)
  blocking collectives  187 us (28%)
  local copies, waits for them, and re-layouts  164 us (25%)
  other arithmetic  62.1 us (9%)
  matrix products  26.2 us (4%)
  between operations  14.7 us (2%)
    all_gather x1, waiting for transfers between devices, per_device(): gathered = lax.all_gather(turned, 'bl', axis=0, tiled=True)  200 us
    all_to_all x1, blocking collectives, per_device(): lax.all_to_all(spectra, 'freq', split_axis=3, concat_axis=0, tiled=True)  187 us
    reshape x2, local copies, waits for them, and re-layouts, per_device(): spectra = (spectra * (1.0 / math.sqrt(K))).astype(jnp.bfloat16).reshape(l...  42.6 us
    transpose x3, local copies, waits for them, and re-layouts, arrange(): jnp.transpose(panel, (3, 0, 2, 1))  39.3 us
    reshape x2, local copies, waits for them, and re-layouts, arrange(): jnp.transpose(panel, (3, 0, 2, 1))  28.2 us
    all_to_all x2, local copies, waits for them, and re-layouts, per_device(): lax.all_to_all(spectra, 'freq', split_axis=3, concat_axis=0, tiled=True)  26.3 us
    transpose x3, other arithmetic, arrange(): jnp.transpose(panel, (3, 0, 2, 1))  21.5 us
    convert_element_type x1, other arithmetic, per_device(): filtered = filtered.astype(jnp.bfloat16)  19.3 us
  transfers between devices with their start and end apart: 1, of which 1 were waited for; matrix products, arithmetic and copies ran while one was open for 0% of the time, Pallas kernels for 0%

commit v1 on v0

--- a/solution.py
+++ b/solution.py
@@ -1,14 +1,22 @@
+import functools
 import math
 
 import jax
 import jax.numpy as jnp
+import numpy as np
 from jax import lax
+from jax.experimental import pallas as pl
+from jax.experimental.pallas import tpu as pltpu
 from jax.sharding import PartitionSpec as P
 
 K = 1024
 TAPS = 4
 PANEL = 256
 SAMPLES = 128
+LANES = 128
+WIDE = 16
+NARROW = 8
+MESH = pl.DeviceIdType.MESH
 
 
 def make_table(points, kept):
@@ -31,17 +39,22 @@
     return arrange(turned)
 
 
+def picked(source, ids):
+    pick = (ids[:, None] == jnp.arange(source.shape[0], dtype=jnp.int32)[None, :]).astype(jnp.bfloat16)
+    return jnp.einsum("at,tspf->aspf", pick, source, preferred_element_type=jnp.float32).astype(jnp.bfloat16)
+
+
 def correlate(source, antenna_order, tile):
     row_ids = lax.dynamic_slice_in_dim(antenna_order, tile[0] * PANEL, PANEL)
     col_ids = lax.dynamic_slice_in_dim(antenna_order, tile[1] * PANEL, PANEL)
-    row_panel = jnp.take(source, row_ids, axis=0)
-    col_panel = jnp.take(source, col_ids, axis=0)
+    row_panel = picked(source, row_ids)
+    col_panel = picked(source, col_ids)
     left = arrange(row_panel)
     right = jnp.concatenate([arrange(col_panel), rotated(col_panel)], axis=1)
     return jnp.einsum("fps,fqs->fpq", left, right, preferred_element_type=jnp.float32)
 
 
-def per_device(voltages, fir_taps, antenna_order, tile_list):
+def per_device_plain(voltages, fir_taps, antenna_order, tile_list):
     local_count = voltages.shape[0]
     frames = voltages.reshape(local_count, SAMPLES + TAPS - 1, K)
     filtered = jnp.zeros((local_count, SAMPLES, K), jnp.float32)
@@ -66,9 +79,247 @@
     return (summed / SAMPLES).astype(jnp.bfloat16)[None]
 
 
+def chunked_table(groups, width):
+    m = np.arange(K)[None, :] * np.arange(K // 2)[:, None] % K
+    phase = 2.0 * math.pi / K * m
+    table = np.stack([np.cos(phase), -np.sin(phase)])
+    table = table.reshape(2, groups, -1, width, K).transpose(2, 0, 1, 3, 4)
+    return table.reshape(table.shape[0], 2 * groups * width, K).astype(jnp.bfloat16)
+
+
+def spectra_kernel(
+    groups, tiles, volt_ref, taps_ref, table_ref, all_ref,
+    filt32, filt, turn, send, own_sem, s1, r1, s2, r2, s3, r3, s4, r4,
+):
+    me = lax.axis_index("freq")
+    bl = lax.axis_index("bl")
+    core = bl % 2
+    mate = bl + 1 - 2 * core
+    across = [(bl + 2 * e) % tiles for e in range(1, tiles // 2)]
+    ants = volt_ref.shape[0]
+    block = groups * ants
+
+    barrier = pltpu.get_barrier_semaphore()
+    for d in range(1, groups):
+        pl.semaphore_signal(barrier, inc=1, device_id={"freq": (me + d) % groups}, device_id_type=MESH)
+    for there in (mate, *across):
+        pl.semaphore_signal(barrier, inc=1, device_id={"bl": there}, device_id_type=MESH)
+    pl.semaphore_wait(barrier, groups - 1 + 1 + len(across))
+
+    @pl.loop(0, SAMPLES // 8)
+    def _(step):
+        for half in range(K // 256):
+            cols = 256 * half
+            taps = [taps_ref[t : t + 1, cols : cols + 256] for t in range(TAPS)]
+            frames = []
+            for i in range(8 + TAPS - 1):
+                at = pl.multiple_of((step * 8 + i) * K, K) + cols
+                frames.append(volt_ref[:, pl.ds(pl.multiple_of(at, 256), 256)].astype(jnp.float32))
+            for i in range(8):
+                total = taps[0] * frames[i]
+                for t in range(1, TAPS):
+                    total = total + taps[t] * frames[i + t]
+                for q in range(2):
+                    filt32[2 * half + q, pl.ds(step * 8 + i, ants, stride=SAMPLES), :] = total[
+                        :, q * LANES : (q + 1) * LANES
+                    ]
+
+    @pl.loop(0, ants)
+    def _(a):
+        rows = pl.ds(pl.multiple_of(a * SAMPLES, SAMPLES), SAMPLES)
+        for q in range(K // LANES):
+            filt[rows, q * LANES : (q + 1) * LANES] = filt32[q, rows, :].astype(jnp.bfloat16)
+
+    steps = table_ref.shape[0]
+    per = WIDE // NARROW
+    rows_of = groups * WIDE
+
+    def turn_copies(c):
+        h, w = c % per, c // per
+        copies = []
+        for d in range(1, groups):
+            to = (me + d) % groups
+            copies.append(
+                pltpu.make_async_remote_copy(
+                    src_ref=send.at[w, pl.ds(to * WIDE + h * NARROW, NARROW)],
+                    dst_ref=all_ref.at[
+                        pl.ds(c * NARROW, NARROW), pl.ds(pl.multiple_of(bl * block + me * ants, ants), ants)
+                    ],
+                    send_sem=s1.at[c, d],
+                    recv_sem=r1.at[c, d],
+                    device_id={"freq": to},
+                    device_id_type=MESH,
+                )
+            )
+        own = pltpu.make_async_copy(
+            send.at[w, pl.ds(me * WIDE + h * NARROW, NARROW)],
+            all_ref.at[pl.ds(c * NARROW, NARROW), pl.ds(pl.multiple_of(bl * block + me * ants, ants), ants)],
+            own_sem.at[c],
+        )
+        return copies, own
+
+    def block_of(c, b):
+        return all_ref.at[pl.ds(c * NARROW, NARROW), pl.ds(pl.multiple_of(b * block, block), block)]
+
+    def block_copy(c, b, there, ssem, rsem):
+        return pltpu.make_async_remote_copy(
+            src_ref=block_of(c, b), dst_ref=block_of(c, b), send_sem=ssem, recv_sem=rsem,
+            device_id={"bl": there}, device_id_type=MESH,
+        )
+
+    def across_copies(c):
+        return [block_copy(c, bl, there, s2.at[c, e], r2.at[c, e]) for e, there in enumerate(across)]
+
+    def mate_copy(c):
+        return block_copy(c, bl, mate, s3.at[c], r3.at[c])
+
+    def passed_copies(c):
+        return [
+            block_copy(c, (bl + tiles - 2 * (e + 1)) % tiles, mate, s4.at[c, e], r4.at[c, e])
+            for e in range(len(across))
+        ]
+
+    chunks = steps * per
+
+    def spread(c):
+        copies, own = turn_copies(c)
+        for copy in copies:
+            copy.wait_recv()
+        own.wait()
+        for copy in across_copies(c):
+            copy.start()
+        mate_copy(c).start()
+
+    def hand_on(c):
+        arrived, passed = across_copies(c), passed_copies(c)
+        for one, two in zip(arrived, passed):
+            one.wait_recv()
+            two.start()
+
+    for w in range(steps):
+
+        @pl.loop(0, ants // 4)
+        def _(q):
+            rows = pl.ds(pl.multiple_of(q * 4 * SAMPLES, 4 * SAMPLES), 4 * SAMPLES)
+            made = lax.dot_general(
+                table_ref[w], filt[rows, :], (((1,), (1,)), ((), ())), preferred_element_type=jnp.float32
+            ) * (1.0 / math.sqrt(K))
+            for i in range(4):
+                for p in range(2):
+                    turn[p, pl.ds(q * 4 + i, rows_of, stride=ants), :] = made[
+                        p * rows_of : (p + 1) * rows_of, i * SAMPLES : (i + 1) * SAMPLES
+                    ]
+
+        @pl.loop(0, rows_of // 8)
+        def _(r):
+            for p in range(2):
+                rows = turn[p, pl.ds(pl.multiple_of(r * 8 * ants, 8 * ants), 8 * ants), :]
+                send[w, pl.ds(pl.multiple_of(r * 8, 8), 8), :, p * LANES : (p + 1) * LANES] = rows.reshape(
+                    8, ants, LANES
+                ).astype(jnp.bfloat16)
+
+        for c in range(w * per, (w + 1) * per):
+            if c >= 2:
+                for copy in turn_copies(c - 2)[0]:
+                    copy.wait_send()
+            copies, own = turn_copies(c)
+            own.start()
+            for copy in copies:
+                copy.start()
+            if c >= 2:
+                spread(c - 2)
+            if c >= 4:
+                hand_on(c - 4)
+    for c in range(chunks - 2, chunks):
+        spread(c)
+    for c in range(chunks - 4, chunks):
+        hand_on(c)
+    for c in range(chunks):
+        mate_copy(c).wait()
+        for copy in across_copies(c):
+            copy.wait_send()
+        for copy in passed_copies(c):
+            copy.wait()
+    for c in range(chunks - 2, chunks):
+        for copy in turn_copies(c)[0]:
+            copy.wait_send()
+
+
+def correlate_kernel(pick_ref, all_ref, out_ref):
+    for f in range(all_ref.shape[0]):
+        both = jnp.dot(pick_ref[...], all_ref[f], preferred_element_type=jnp.float32).astype(jnp.bfloat16)
+        left, right = both[:PANEL], both[PANEL:]
+        turned = jnp.concatenate([-right[:, SAMPLES:], right[:, :SAMPLES]], axis=1)
+        for at, other in enumerate((right, turned)):
+            summed = lax.dot_general(left, other, (((1,), (1,)), ((), ())), preferred_element_type=jnp.float32)
+            out_ref[f, :, at * PANEL : (at + 1) * PANEL] = (summed * (1.0 / SAMPLES)).astype(jnp.bfloat16)
+
+
+def per_device(groups, tiles, voltages, fir_taps, antenna_order, tile_list):
+    ants = voltages.shape[0]
+    total = ants * groups * tiles
+    channels = K // 2 // groups
+    table = jnp.asarray(chunked_table(groups, WIDE))
+    steps = channels // WIDE
+    chunks = channels // NARROW
+    others = max(tiles // 2 - 1, 1)
+    dma = pltpu.SemaphoreType.DMA
+    gathered = pl.pallas_call(
+        functools.partial(spectra_kernel, groups, tiles),
+        out_shape=jax.ShapeDtypeStruct((channels, total, 2 * SAMPLES), jnp.bfloat16),
+        in_specs=[pl.BlockSpec(memory_space=pltpu.VMEM)] * 3,
+        out_specs=pl.BlockSpec(memory_space=pl.ANY),
+        scratch_shapes=[
+            pltpu.VMEM((K // LANES, ants * SAMPLES, LANES), jnp.float32),
+            pltpu.VMEM((ants * SAMPLES, K), jnp.bfloat16),
+            pltpu.VMEM((2, groups * WIDE * ants, LANES), jnp.float32),
+            pltpu.VMEM((steps, groups * WIDE, ants, 2 * SAMPLES), jnp.bfloat16),
+            dma((chunks,)),
+            dma((chunks, groups)), dma((chunks, groups)),
+            dma((chunks, others)), dma((chunks, others)),
+            dma((chunks,)), dma((chunks,)),
+            dma((chunks, others)), dma((chunks, others)),
+        ],
+        cost_estimate=pl.CostEstimate(flops=10**10, bytes_accessed=10**8, transcendentals=0),
+        compiler_params=pltpu.CompilerParams(
+            collective_id=0, has_side_effects=True, vmem_limit_bytes=58 * 2**20
+        ),
+        name="spectra",
+    )(voltages, fir_taps, table)
+
+    tile = tile_list[lax.axis_index("bl")]
+    ids = jnp.concatenate(
+        [lax.dynamic_slice_in_dim(antenna_order, tile[i] * PANEL, PANEL) for i in range(2)]
+    )
+    pick = (ids[:, None] == jnp.arange(total, dtype=jnp.int32)[None, :]).astype(jnp.bfloat16)
+    at_once = 4
+    seen = pl.pallas_call(
+        correlate_kernel,
+        grid=(channels // at_once,),
+        out_shape=jax.ShapeDtypeStruct((channels, PANEL, 2 * PANEL), jnp.bfloat16),
+        in_specs=[
+            pl.BlockSpec((2 * PANEL, total), lambda i: (0, 0)),
+            pl.BlockSpec((at_once, total, 2 * SAMPLES), lambda i: (i, 0, 0)),
+        ],
+        out_specs=pl.BlockSpec((at_once, PANEL, 2 * PANEL), lambda i: (i, 0, 0)),
+        compiler_params=pltpu.CompilerParams(vmem_limit_bytes=32 * 2**20),
+        name="correlate",
+    )(pick, gathered)
+    return seen[None]
+
+
 def solution(mesh):
+    groups, tiles = mesh.shape["freq"], mesh.shape["bl"]
+
+    def run(voltages, fir_taps, antenna_order, tile_list):
+        if voltages.shape[0] % 16 == 0 and (K // 2 // groups) % WIDE == 0 and tiles % 2 == 0:
+            body = functools.partial(per_device, groups, tiles)
+        else:
+            body = per_device_plain
+        return body(voltages, fir_taps, antenna_order, tile_list)
+
     return jax.shard_map(
-        per_device,
+        run,
         mesh=mesh,
         in_specs=(P(("bl", "freq"), None), P(), P(), P()),
         out_specs=P("bl", "freq", None, None),

time: 659 us -> 337 us (0.51)
  Pallas kernels: 0 us -> 332 us
  waiting for transfers between devices: 200 us -> 0 us
  blocking collectives: 187 us -> 0 us
  local copies, waits for them, and re-layouts: 164 us -> 2.18 us
  other arithmetic: 62.1 us -> 0.25 us
  matrix products: 26.2 us -> 0 us
  between operations: 14.7 us -> 1.31 us
    pallas_call x0 -> x2, Pallas kernels: none -> 332 us  [the longest x1 276 us: per_device(): pl.pallas_call(functools.partial(spectra_kernel, groups, tiles), out_shap...]
    all_gather x1 -> x0, waiting for transfers between devices: 200 us -> none  [per_device(): gathered = lax.all_gather(turned, 'bl', axis=0, tiled=True)]
    all_to_all x1 -> x0, blocking collectives: 187 us -> none  [per_device(): lax.all_to_all(spectra, 'freq', split_axis=3, concat_axis=0, tiled=True)]
    reshape x5 -> x0, local copies, waits for them, and re-layouts: 80 us -> none  [the longest x2 42.6 us: per_device(): spectra = (spectra * (1.0 / math.sqrt(K))).astype(jnp.bfloat16).reshape(l...]
    transpose x3 -> x0, local copies, waits for them, and re-layouts: 39.3 us -> none  [arrange(): jnp.transpose(panel, (3, 0, 2, 1))]
    all_to_all x2 -> x0, local copies, waits for them, and re-layouts: 26.3 us -> none  [per_device(): lax.all_to_all(spectra, 'freq', split_axis=3, concat_axis=0, tiled=True)]
    dot_general x2 -> x0, matrix products: 26.2 us -> none  [the longest x1 15.2 us: correlate(): jnp.einsum('fps,fqs->fpq', left, right, preferred_element_type=jnp.float32)]
    transpose x3 -> x0, other arithmetic: 21.5 us -> none  [arrange(): jnp.transpose(panel, (3, 0, 2, 1))]
  transfers between devices with their start and end apart: 1 -> 0, of which waited for: 1 -> 0; matrix products, arithmetic and copies ran while one was open for 0% -> 0% of each run, Pallas kernels for 0% -> 0%
where the time goes in v1:
time: 337 us; the launch traced here: 336 us
  Pallas kernels  332 us (99%)
    pallas_call x1, Pallas kernels, per_device(): pl.pallas_call(functools.partial(spectra_kernel, groups, tiles), out_shap...  276 us
    pallas_call x1, Pallas kernels, per_device(): pl.pallas_call(correlate_kernel, grid=(channels // at_once,), out_shape=j...  56 us

profile of v1, /device:TPU:10, one launch (start us, length us, event | category | flops | bytes accessed | tf_op | source)
XLA Modules:
  0.0 335.7 jit_solution(4856630498185739867)
XLA Ops:
  0.0 0.0 copy-start
  0.0 0.7 copy-done
  0.7 0.1 constant_dynamic-slice_fusion
  0.8 0.6 fusion.2
  2.6 0.8 fusion.1
  3.5 0.2 fusion.pick_ref
  3.7 275.9 %spectra.1.all_ref = bf16[64,1024,256]{2,1,0:T(8,128)(2,1)} custom-call(bf16[32,134144]{1,0:T(8,128)(2,1)} %volt_ref.1, f32[4,1024]{1,0:T(4,128)} %taps_ref.1, bf16[4,256,1024]{2,1,0:T(8,128)(2,1)} %constant.16.clone.table_ref), custom_call_target="tpu_custom_call" | custom-call | flops 10000000000 | bytes 100000000 | tf_op jit(solution)/shard_map/spectra/pallas_call | solution.py:267
  279.7 56.0 %correlate.1 = bf16[64,256,512]{2,1,0:T(8,128)(2,1)} custom-call(bf16[512,1024]{1,0:T(8,128)(2,1)S(1)} %fusion.pick_ref, bf16[64,1024,256]{2,1,0:T(8,128)(2,1)} %spectra.1.all_ref), custom_call_target="tpu_custom_call" | custom-call | tf_op jit(solution)/shard_map/correlate/pallas_call | solution.py:296
  (1 shorter events, 0.0 us)
Async XLA Ops:
  0.0 0.7 copy-start

commit v2 on v1

--- a/solution.py
+++ b/solution.py
@@ -15,7 +15,8 @@
 SAMPLES = 128
 LANES = 128
 WIDE = 16
-NARROW = 8
+NARROW = 4
+AHEAD = 3
 MESH = pl.DeviceIdType.MESH
 
 
@@ -88,8 +89,8 @@
 
 
 def spectra_kernel(
-    groups, tiles, volt_ref, taps_ref, table_ref, all_ref,
-    filt32, filt, turn, send, own_sem, s1, r1, s2, r2, s3, r3, s4, r4,
+    groups, tiles, volt_ref, taps_ref, table_ref, pick_ref, seen_ref, all_ref,
+    filt32, filt, turn, send, held, made_vis, held_sem, seen_sem, own_sem, s1, r1, s2, r2, s3, r3, s4, r4,
 ):
     me = lax.axis_index("freq")
     bl = lax.axis_index("bl")
@@ -196,6 +197,41 @@
             one.wait_recv()
             two.start()
 
+    def seen_copy(c):
+        return pltpu.make_async_copy(made_vis, seen_ref.at[pl.ds(c * NARROW, NARROW)], seen_sem)
+
+    def products(c):
+        mate_copy(c).wait_recv()
+        for copy in passed_copies(c):
+            copy.wait_recv()
+        load = pltpu.make_async_copy(all_ref.at[pl.ds(c * NARROW, NARROW)], held, held_sem)
+        load.start()
+        if c >= 1:
+            seen_copy(c - 1).wait()
+        load.wait()
+
+        @pl.loop(0, NARROW)
+        def _(f):
+            correlate_one(pick_ref, held, made_vis, f)
+
+        seen_copy(c).start()
+
+    def advance(c):
+        if 0 <= c - AHEAD < chunks:
+            for copy in turn_copies(c - AHEAD)[0]:
+                copy.wait_send()
+        if c < chunks:
+            copies, own = turn_copies(c)
+            own.start()
+            for copy in copies:
+                copy.start()
+        if 0 <= c - AHEAD < chunks:
+            spread(c - AHEAD)
+        if 0 <= c - AHEAD - 1 < chunks:
+            hand_on(c - AHEAD - 1)
+        if 0 <= c - AHEAD - 2 < chunks:
+            products(c - AHEAD - 2)
+
     for w in range(steps):
 
         @pl.loop(0, ants // 4)
@@ -219,40 +255,23 @@
                 ).astype(jnp.bfloat16)
 
         for c in range(w * per, (w + 1) * per):
-            if c >= 2:
-                for copy in turn_copies(c - 2)[0]:
-                    copy.wait_send()
-            copies, own = turn_copies(c)
-            own.start()
-            for copy in copies:
-                copy.start()
-            if c >= 2:
-                spread(c - 2)
-            if c >= 4:
-                hand_on(c - 4)
-    for c in range(chunks - 2, chunks):
-        spread(c)
-    for c in range(chunks - 4, chunks):
-        hand_on(c)
+            advance(c)
+    for c in range(chunks, chunks + AHEAD + 2):
+        advance(c)
+    seen_copy(chunks - 1).wait()
     for c in range(chunks):
-        mate_copy(c).wait()
-        for copy in across_copies(c):
+        mate_copy(c).wait_send()
+        for copy in (*across_copies(c), *passed_copies(c)):
             copy.wait_send()
-        for copy in passed_copies(c):
-            copy.wait()
-    for c in range(chunks - 2, chunks):
-        for copy in turn_copies(c)[0]:
-            copy.wait_send()
-
-
-def correlate_kernel(pick_ref, all_ref, out_ref):
-    for f in range(all_ref.shape[0]):
-        both = jnp.dot(pick_ref[...], all_ref[f], preferred_element_type=jnp.float32).astype(jnp.bfloat16)
-        left, right = both[:PANEL], both[PANEL:]
-        turned = jnp.concatenate([-right[:, SAMPLES:], right[:, :SAMPLES]], axis=1)
-        for at, other in enumerate((right, turned)):
-            summed = lax.dot_general(left, other, (((1,), (1,)), ((), ())), preferred_element_type=jnp.float32)
-            out_ref[f, :, at * PANEL : (at + 1) * PANEL] = (summed * (1.0 / SAMPLES)).astype(jnp.bfloat16)
+
+
+def correlate_one(pick_ref, held, out_ref, f):
+    both = jnp.dot(pick_ref[...], held[f], preferred_element_type=jnp.float32).astype(jnp.bfloat16)
+    left, right = both[:PANEL], both[PANEL:]
+    turned = jnp.concatenate([-right[:, SAMPLES:], right[:, :SAMPLES]], axis=1)
+    for at, other in enumerate((right, turned)):
+        summed = lax.dot_general(left, other, (((1,), (1,)), ((), ())), preferred_element_type=jnp.float32)
+        out_ref[f, :, at * PANEL : (at + 1) * PANEL] = (summed * (1.0 / SAMPLES)).astype(jnp.bfloat16)
 
 
 def per_device(groups, tiles, voltages, fir_taps, antenna_order, tile_list):
@@ -264,16 +283,27 @@
     chunks = channels // NARROW
     others = max(tiles // 2 - 1, 1)
     dma = pltpu.SemaphoreType.DMA
-    gathered = pl.pallas_call(
+    tile = tile_list[lax.axis_index("bl")]
+    ids = jnp.concatenate(
+        [lax.dynamic_slice_in_dim(antenna_order, tile[i] * PANEL, PANEL) for i in range(2)]
+    )
+    pick = (ids[:, None] == jnp.arange(total, dtype=jnp.int32)[None, :]).astype(jnp.bfloat16)
+    seen, _ = pl.pallas_call(
         functools.partial(spectra_kernel, groups, tiles),
-        out_shape=jax.ShapeDtypeStruct((channels, total, 2 * SAMPLES), jnp.bfloat16),
-        in_specs=[pl.BlockSpec(memory_space=pltpu.VMEM)] * 3,
-        out_specs=pl.BlockSpec(memory_space=pl.ANY),
+        out_shape=(
+            jax.ShapeDtypeStruct((channels, PANEL, 2 * PANEL), jnp.bfloat16),
+            jax.ShapeDtypeStruct((channels, total, 2 * SAMPLES), jnp.bfloat16),
+        ),
+        in_specs=[pl.BlockSpec(memory_space=pltpu.VMEM)] * 4,
+        out_specs=(pl.BlockSpec(memory_space=pl.ANY),) * 2,
         scratch_shapes=[
             pltpu.VMEM((K // LANES, ants * SAMPLES, LANES), jnp.float32),
             pltpu.VMEM((ants * SAMPLES, K), jnp.bfloat16),
             pltpu.VMEM((2, groups * WIDE * ants, LANES), jnp.float32),
             pltpu.VMEM((steps, groups * WIDE, ants, 2 * SAMPLES), jnp.bfloat16),
+            pltpu.VMEM((NARROW, total, 2 * SAMPLES), jnp.bfloat16),
+            pltpu.VMEM((NARROW, PANEL, 2 * PANEL), jnp.bfloat16),
+            dma, dma,
             dma((chunks,)),
             dma((chunks, groups)), dma((chunks, groups)),
             dma((chunks, others)), dma((chunks, others)),
@@ -285,26 +315,7 @@
             collective_id=0, has_side_effects=True, vmem_limit_bytes=58 * 2**20
         ),
         name="spectra",
-    )(voltages, fir_taps, table)
-
-    tile = tile_list[lax.axis_index("bl")]
-    ids = jnp.concatenate(
-        [lax.dynamic_slice_in_dim(antenna_order, tile[i] * PANEL, PANEL) for i in range(2)]
-    )
-    pick = (ids[:, None] == jnp.arange(total, dtype=jnp.int32)[None, :]).astype(jnp.bfloat16)
-    at_once = 4
-    seen = pl.pallas_call(
-        correlate_kernel,
-        grid=(channels // at_once,),
-        out_shape=jax.ShapeDtypeStruct((channels, PANEL, 2 * PANEL), jnp.bfloat16),
-        in_specs=[
-            pl.BlockSpec((2 * PANEL, total), lambda i: (0, 0)),
-            pl.BlockSpec((at_once, total, 2 * SAMPLES), lambda i: (i, 0, 0)),
-        ],
-        out_specs=pl.BlockSpec((at_once, PANEL, 2 * PANEL), lambda i: (i, 0, 0)),
-        compiler_params=pltpu.CompilerParams(vmem_limit_bytes=32 * 2**20),
-        name="correlate",
-    )(pick, gathered)
+    )(voltages, fir_taps, table, pick)
     return seen[None]
 
 

time: 337 us -> 280 us (0.83)
  Pallas kernels: 332 us -> 260 us
  local copies, waits for them, and re-layouts: 2.18 us -> 15.9 us
    pallas_call x1 -> x0, Pallas kernels: 56 us -> none  [per_device(): pl.pallas_call(correlate_kernel, grid=(channels // at_once,), out_shape=j...]
    pallas_call x1, Pallas kernels: 276 us -> 260 us  [per_device(): pl.pallas_call(functools.partial(spectra_kernel, groups, tiles), out_shap...]
    unnamed x2 -> x5, local copies, waits for them, and re-layouts: 0.68 us -> 14.5 us
where the time goes in v2:
time: 280 us; the launch traced here: 279 us
  Pallas kernels  260 us (93%)
  local copies, waits for them, and re-layouts  15.9 us (6%)
    pallas_call x1, Pallas kernels, per_device(): pl.pallas_call(functools.partial(spectra_kernel, groups, tiles), out_shap...  260 us
    unnamed x5, local copies, waits for them, and re-layouts  14.5 us

profile of v2, /device:TPU:10, one launch (start us, length us, event | category | flops | bytes accessed | tf_op | source)
XLA Modules:
  0.0 278.9 jit_solution(1907493895067009717)
XLA Ops:
  0.0 0.0 copy-start
  0.0 0.7 copy-done
  0.7 0.1 constant_dynamic-slice_fusion
  0.8 0.5 fusion.2
  2.6 0.8 fusion.1
  3.4 1.2 fusion.pick_ref
  4.6 260.5 %spectra.1 = (bf16[64,256,512]{2,1,0:T(8,128)(2,1)}, bf16[64,1024,256]{2,1,0:T(8,128)(2,1)}) custom-call(bf16[32,134144]{1,0:T(8,128)(2,1)} %volt_ref.1, f32[4,1024]{1,0:T(4,128)} %taps_ref.1, bf16[4,256,1024]{2,1,0:T(8,128)(2,1)} %constant.16.clone.table_ref, bf16[512,1024]{1,0:T(8,128)(2,1)} %fusion.pick_ref), custom_call_target="tpu_custom_call" | custom-call | flops 10000000000 | bytes 100000000 | tf_op jit(solution)/shard_map/spectra/pallas_call | solution.py:291
  265.1 0.0 copy-start.1
  265.1 13.8 %copy.7 = bf16[1,64,256,512]{3,2,1,0:T(8,128)(2,1)} copy(bf16[1,64,256,512]{3,2,1,0:T(8,128)(2,1)} %bitcast.3) | data formatting | bytes 33554432
  278.9 0.0 copy-done.1
  (1 shorter events, 0.0 us)
Async XLA Ops:
  0.0 0.7 copy-start
  265.1 13.8 %copy-start.1 = (s32[4,2]{0,1:T(2,128)S(1)}, s32[4,2]{0,1:T(2,128)}, u32[]{:S(2)}) copy-start(s32[4,2]{0,1:T(2,128)} %param.8) | copy-start | bytes 100

commit v3 on v2

--- a/solution.py
+++ b/solution.py
@@ -16,7 +16,7 @@
 LANES = 128
 WIDE = 16
 NARROW = 4
-AHEAD = 3
+AHEAD = 2
 MESH = pl.DeviceIdType.MESH
 
 
@@ -217,8 +217,9 @@
         seen_copy(c).start()
 
     def advance(c):
-        if 0 <= c - AHEAD < chunks:
-            for copy in turn_copies(c - AHEAD)[0]:
+        sent = 0 if c == 1 else c - AHEAD
+        if (sent > 0 or c == 1) and sent < chunks:
+            for copy in turn_copies(sent)[0]:
                 copy.wait_send()
         if c < chunks:
             copies, own = turn_copies(c)

time: 280 us -> 274 us (0.979)
  Pallas kernels: 260 us -> 255 us
    pallas_call x1, Pallas kernels: 260 us -> 255 us  [per_device(): pl.pallas_call(functools.partial(spectra_kernel, groups, tiles), out_shap...]
where the time goes in v3:
time: 274 us
  Pallas kernels  255 us (93%)
  local copies, waits for them, and re-layouts  15.9 us (6%)
    pallas_call x1, Pallas kernels, per_device(): pl.pallas_call(functools.partial(spectra_kernel, groups, tiles), out_shap...  255 us
    unnamed x5, local copies, waits for them, and re-layouts  14.5 us

profile of v3, /device:TPU:10, one launch (start us, length us, event | category | flops | bytes accessed | tf_op | source)
XLA Modules:
  0.0 273.6 jit_solution(12333621886887103721)
XLA Ops:
  0.0 0.0 copy-start
  0.0 0.7 copy-done
  0.7 0.1 constant_dynamic-slice_fusion
  0.8 0.5 fusion.2
  2.6 0.8 fusion.1
  3.4 1.2 fusion.pick_ref
  4.6 255.2 %spectra.1 = (bf16[64,256,512]{2,1,0:T(8,128)(2,1)}, bf16[64,1024,256]{2,1,0:T(8,128)(2,1)}) custom-call(bf16[32,134144]{1,0:T(8,128)(2,1)} %volt_ref.1, f32[4,1024]{1,0:T(4,128)} %taps_ref.1, bf16[4,256,1024]{2,1,0:T(8,128)(2,1)} %constant.16.clone.table_ref, bf16[512,1024]{1,0:T(8,128)(2,1)} %fusion.pick_ref), custom_call_target="tpu_custom_call" | custom-call | flops 10000000000 | bytes 100000000 | tf_op jit(solution)/shard_map/spectra/pallas_call | solution.py:292
  259.8 0.0 copy-start.1
  259.8 13.8 %copy.7 = bf16[1,64,256,512]{3,2,1,0:T(8,128)(2,1)} copy(bf16[1,64,256,512]{3,2,1,0:T(8,128)(2,1)} %bitcast.3) | data formatting | bytes 33554432
  273.6 0.0 copy-done.1
  (1 shorter events, 0.0 us)
Async XLA Ops:
  0.0 0.7 copy-start
  259.8 13.8 %copy-start.1 = (s32[4,2]{0,1:T(2,128)S(1)}, s32[4,2]{0,1:T(2,128)}, u32[]{:S(2)}) copy-start(s32[4,2]{0,1:T(2,128)} %param.8) | copy-start | bytes 100

commit v4 on v3

--- a/solution.py
+++ b/solution.py
@@ -14,7 +14,7 @@
 PANEL = 256
 SAMPLES = 128
 LANES = 128
-WIDE = 16
+WIDE = 8
 NARROW = 4
 AHEAD = 2
 MESH = pl.DeviceIdType.MESH

time: 274 us -> 273 us (level)
  no operation moved by 1% of the time
where the time goes in v4:
time: 273 us; the launch traced here: 272 us
  Pallas kernels  254 us (93%)
  local copies, waits for them, and re-layouts  15.9 us (6%)
    pallas_call x1, Pallas kernels, per_device(): pl.pallas_call(functools.partial(spectra_kernel, groups, tiles), out_shap...  254 us
    unnamed x5, local copies, waits for them, and re-layouts  14.5 us

profile of v4, /device:TPU:10, one launch (start us, length us, event | category | flops | bytes accessed | tf_op | source)
XLA Modules:
  0.0 272.4 jit_solution(527163192466854722)
XLA Ops:
  0.0 0.0 copy-start
  0.0 0.7 copy-done
  0.7 0.1 constant_dynamic-slice_fusion
  0.8 0.5 fusion.2
  2.6 0.8 fusion.1
  3.4 1.2 fusion.pick_ref
  4.6 254.0 %spectra.1 = (bf16[64,256,512]{2,1,0:T(8,128)(2,1)}, bf16[64,1024,256]{2,1,0:T(8,128)(2,1)}) custom-call(bf16[32,134144]{1,0:T(8,128)(2,1)} %volt_ref.1, f32[4,1024]{1,0:T(4,128)} %taps_ref.1, bf16[8,128,1024]{2,1,0:T(8,128)(2,1)} %constant.16.clone.table_ref, bf16[512,1024]{1,0:T(8,128)(2,1)} %fusion.pick_ref), custom_call_target="tpu_custom_call" | custom-call | flops 10000000000 | bytes 100000000 | tf_op jit(solution)/shard_map/spectra/pallas_call | solution.py:292
  258.6 0.0 copy-start.1
  258.7 13.8 %copy.7 = bf16[1,64,256,512]{3,2,1,0:T(8,128)(2,1)} copy(bf16[1,64,256,512]{3,2,1,0:T(8,128)(2,1)} %bitcast.3) | data formatting | bytes 33554432
  272.4 0.0 copy-done.1
  (1 shorter events, 0.0 us)
Async XLA Ops:
  0.0 0.7 copy-start
  258.6 13.8 %copy-start.1 = (s32[4,2]{0,1:T(2,128)S(1)}, s32[4,2]{0,1:T(2,128)}, u32[]{:S(2)}) copy-start(s32[4,2]{0,1:T(2,128)} %param.8) | copy-start | bytes 100
